TPU v7x, 32 devices: a whole 2x2x4 slice. The times are simulated.
32 devices in a mesh: segment: 2 (over core), dp: 8 (over z, x), mp: 2 (over y).
Axes of the slice: x: 2, y: 2, z: 4, core: 2. Of those that a mesh axis runs over, the one named last changes fastest.
Arguments:
- grad_top: bfloat16 [4096, 2048], P('dp'), may hold values from -6 to 6
- saved_query: bfloat16 [2, 4096, 2048], P('segment', 'dp', 'mp'), may hold values from -12 to 12
- saved_key: bfloat16 [2, 6144, 2048], P('segment', 'dp', 'mp'), may hold values from -4 to 4
- saved_value: bfloat16 [2, 6144, 2048], P('segment', 'dp', 'mp'), may hold values from -6 to 6
- w_query: bfloat16 [2, 2048, 2048], P('segment', 'mp', 'dp'), may hold values from -0.125 to 0.125
- w_key: bfloat16 [2, 2048, 2048], P('segment', 'mp', 'dp'), may hold values from -0.125 to 0.125
- w_value: bfloat16 [2, 2048, 2048], P('segment', 'mp', 'dp'), may hold values from -0.125 to 0.125
- w_out: bfloat16 [2, 2048, 2048], P('segment', 'mp', 'dp'), may hold values from -0.125 to 0.125
- query_length: int32 [16, 2], P('dp'), may hold values from 64 to 128
- key_offset: int32 [16, 2], P('dp'), may hold values from 0 to 2, as said below
- key_length: int32 [16, 2], P('dp'), may hold values from 64 to 256
- tile_owner: int32 [16, 3], replicated, may hold values from 0 to 47, as said below
Outputs:
- section_grads: bfloat16 [2, 4096, 2048], P('segment', 'dp', 'mp')
- encoder_grads: bfloat16 [6144, 2048], P('dp', ('segment', 'mp'))
Inputs may be any that keep to these rules, and one draw needn't show every extreme that they name: Example 0 takes tiles 0 to key_offset[s, 1] - 1 and example 1 the rest of the sequence's encoder tiles; each example holds at least one tile and its rows fit in its tiles. `tile_owner`: every global tile appears once. Tile t is owned by dp index t // 6; the owner of a tile of dp index i (sequences i * 2 to i * 2 + 1) is i - 1, i or i + 1, wrapping around. Each dp index hands 1 to 2 tiles to each neighbour, and 2 is reached in every draw.
All inputs are finite; a program needn't handle non-finite values.
Results may differ from a plain program's by a relative error of at most 0.019.
Values may be sent and summed in bfloat16 or wider, within the bound.
A program may use at most 128 MiB of HBM per device.

v0:
```python
import jax
import jax.numpy as jnp
from jax import lax
from jax.sharding import PartitionSpec as P

DH = 256
TILE = 128
CAP = 2
masked_floor = -1e30


def shifted(block, axis, distance):
    devices = range(lax.axis_size(axis))
    route = [(i - distance, i) for i in devices if i - distance in devices]
    return lax.ppermute(block, axis, route)


def extended_2(block, sides, width):
    for axis, dim in sides:
        count = lax.axis_size(axis)
        forward = [(i, i + 1) for i in range(count - 1)]
        forward.append((count - 1, 0))
        backward = [(target, source) for source, target in forward]
        low = lax.ppermute(
            lax.slice_in_dim(block, block.shape[dim] - width, None, axis=dim), axis, forward
        )
        high = lax.ppermute(lax.slice_in_dim(block, 0, width, axis=dim), axis, backward)
        block = jnp.concatenate([low, block, high], axis=dim)
    return block


def example_mask(query_length, key_offset, key_length, q_rows, k_rows):
    row_ids = jnp.arange(q_rows, dtype=jnp.int32)[:, None]
    starts = jnp.arange(query_length.shape[0], dtype=jnp.int32)[None, :] * TILE
    inside_q = (row_ids >= starts) & (row_ids < starts + query_length[None, :])
    col_ids = jnp.arange(k_rows, dtype=jnp.int32)[:, None]
    key_start = key_offset[None, :] * TILE
    inside_k = (col_ids >= key_start) & (col_ids < key_start + key_length[None, :])
    return jnp.any(inside_q[:, None, :] & inside_k[None, :, :], axis=-1)


def sequence_backward(operands, query_full, out_full):
    grad_in, query_block, key_block, value_block, query_length, key_offset, key_length = operands
    q_rows, local_width = query_block.shape
    k_rows = key_block.shape[0]
    head_count = local_width // DH
    score_scale = DH ** (-0.5)
    out_grad = lax.dot_general(
        grad_in, out_full, (((1,), (1,)), ((), ())), preferred_element_type=jnp.float32
    ).astype(jnp.bfloat16)
    q_heads = query_block.reshape(q_rows, head_count, DH)
    k_heads = key_block.reshape(k_rows, head_count, DH)
    v_heads = value_block.reshape(k_rows, head_count, DH)
    grad_heads = out_grad.reshape(q_rows, head_count, DH)
    scores = (
        jnp.einsum("qhd,khd->hqk", q_heads, k_heads, preferred_element_type=jnp.float32)
        * score_scale
    )
    allowed = example_mask(query_length, key_offset, key_length, q_rows, k_rows)[None]
    masked = jnp.where(allowed, scores, masked_floor)
    row_max = jnp.max(masked, axis=-1, keepdims=True)
    exp_terms = jnp.where(allowed, jnp.exp(masked - row_max), 0.0)
    denominator = jnp.maximum(jnp.sum(exp_terms, axis=-1, keepdims=True), 1.0)
    attention_probs = exp_terms / denominator
    prob_bf = attention_probs.astype(jnp.bfloat16)
    attended = jnp.einsum("hqk,khd->qhd", prob_bf, v_heads, preferred_element_type=jnp.float32)
    out_dot = jnp.sum(grad_heads.astype(jnp.float32) * attended, axis=-1)
    prob_grad = jnp.einsum("qhd,khd->hqk", grad_heads, v_heads, preferred_element_type=jnp.float32)
    score_grad = (attention_probs * (prob_grad - jnp.transpose(out_dot)[:, :, None])).astype(
        jnp.bfloat16
    )
    query_grad = (
        jnp.einsum("hqk,khd->qhd", score_grad, k_heads, preferred_element_type=jnp.float32)
        * score_scale
    ).astype(jnp.bfloat16)
    key_gradient = (
        jnp.einsum("hqk,qhd->khd", score_grad, q_heads, preferred_element_type=jnp.float32)
        * score_scale
    ).astype(jnp.bfloat16)
    value_grad = jnp.einsum(
        "hqk,qhd->khd", prob_bf, grad_heads, preferred_element_type=jnp.float32
    ).astype(jnp.bfloat16)
    mixed_grad = jnp.dot(
        query_grad.reshape(q_rows, local_width), query_full, preferred_element_type=jnp.float32
    )
    return (
        mixed_grad,
        key_gradient.reshape(k_rows, local_width),
        value_grad.reshape(k_rows, local_width),
    )


def ranked(marked):
    ids = jnp.arange(marked.shape[0], dtype=jnp.int32)
    upto = ids[None, :] <= ids[:, None]
    return jnp.sum((upto & marked[None, :]).astype(jnp.int32), axis=1) - 1


def on_device(
    grad_top,
    saved_query,
    saved_key,
    saved_value,
    w_query,
    w_key,
    w_value,
    w_out,
    query_length,
    key_offset,
    key_length,
    tile_owner,
):
    segment_count = lax.axis_size("segment")
    segment_id = lax.axis_index("segment")
    micro_count = query_length.shape[0]
    q_rows = grad_top.shape[0] // micro_count
    k_rows = saved_key.shape[1] // micro_count
    width = grad_top.shape[1]
    local_width = saved_query.shape[2]
    half_width = width // lax.axis_size("mp")
    out_full, query_full, key_full, complete_value = (
        lax.all_gather(w_out[0], "dp", axis=1, tiled=True),
        lax.all_gather(w_query[0], "dp", axis=1, tiled=True),
        lax.all_gather(w_key[0], "dp", axis=1, tiled=True),
        lax.all_gather(w_value[0], "dp", axis=1, tiled=True),
    )

    def run_layer(operands):
        return sequence_backward(operands, query_full, out_full)

    def bypass_layer(operands):
        return (
            jnp.zeros((q_rows, width), jnp.float32),
            jnp.zeros((k_rows, local_width), jnp.bfloat16),
            jnp.zeros((k_rows, local_width), jnp.bfloat16),
        )

    incoming = jnp.zeros((q_rows, width), jnp.bfloat16)
    sections = jnp.zeros((micro_count * q_rows, half_width), jnp.bfloat16)
    key_grads = jnp.zeros((micro_count * k_rows, local_width), jnp.bfloat16)
    value_grads = jnp.zeros((micro_count * k_rows, local_width), jnp.bfloat16)
    for clock_tick in range(micro_count + 1):
        step_id = clock_tick - 1 + segment_id
        active = (step_id >= 0) & (step_id < micro_count)
        picked = jnp.clip(step_id, 0, micro_count - 1)
        top_rows = lax.dynamic_slice_in_dim(grad_top, picked * q_rows, q_rows, 0)
        grad_in = jnp.where(segment_id == segment_count - 1, top_rows, incoming)
        query_block = lax.dynamic_slice_in_dim(saved_query[0], picked * q_rows, q_rows, 0)
        key_block = lax.dynamic_slice_in_dim(saved_key[0], picked * k_rows, k_rows, 0)
        value_block = lax.dynamic_slice_in_dim(saved_value[0], picked * k_rows, k_rows, 0)
        lengths_q = lax.dynamic_index_in_dim(query_length, picked, 0, keepdims=False)
        offsets_k = lax.dynamic_index_in_dim(key_offset, picked, 0, keepdims=False)
        lengths_k = lax.dynamic_index_in_dim(key_length, picked, 0, keepdims=False)
        mixed_grad, key_gradient, value_grad = lax.cond(
            active,
            run_layer,
            bypass_layer,
            (grad_in, query_block, key_block, value_block, lengths_q, offsets_k, lengths_k),
        )
        summed_share = lax.psum_scatter(
            mixed_grad.astype(jnp.bfloat16), "mp", scatter_dimension=1, tiled=True
        ).astype(jnp.float32)
        own_input = lax.dynamic_slice_in_dim(
            grad_in, lax.axis_index("mp") * half_width, half_width, 1
        )
        own_section = (own_input.astype(jnp.float32) + summed_share).astype(jnp.bfloat16)
        if clock_tick < micro_count:
            full_section = lax.all_gather(own_section, "mp", axis=1, tiled=True)
        sections = jnp.where(
            active,
            lax.dynamic_update_slice_in_dim(sections, own_section, picked * q_rows, 0),
            sections,
        )
        key_grads = jnp.where(
            active,
            lax.dynamic_update_slice_in_dim(key_grads, key_gradient, picked * k_rows, 0),
            key_grads,
        )
        value_grads = jnp.where(
            active,
            lax.dynamic_update_slice_in_dim(value_grads, value_grad, picked * k_rows, 0),
            value_grads,
        )
        if clock_tick < micro_count:
            incoming = shifted(full_section, "segment", -1)
    encoder_partial = jnp.dot(key_grads, key_full, preferred_element_type=jnp.float32) + jnp.dot(
        value_grads, complete_value, preferred_element_type=jnp.float32
    )
    reduced = lax.psum_scatter(
        encoder_partial.astype(jnp.bfloat16), ("segment", "mp"), scatter_dimension=1, tiled=True
    )
    tiles_dev = reduced.shape[0] // TILE
    features = reduced.shape[1]
    local_tiles = reduced.reshape(tiles_dev, TILE, features)
    devices = lax.axis_size("dp")
    my_index = lax.axis_index("dp")
    owners_all = tile_owner.reshape(devices, tiles_dev)

    def route_plan(source):
        owner_row = lax.dynamic_index_in_dim(owners_all, source % devices, 0, keepdims=False)
        owner_step = (owner_row // tiles_dev - source % devices + devices) % devices
        return (owner_step, owner_row % tiles_dev)

    mine_step, mine_slot = route_plan(my_index)
    left_step, left_slot = route_plan(my_index - 1 + devices)
    right_step, right_slot = route_plan(my_index + 1)
    capacity_ids = jnp.arange(CAP, dtype=jnp.int32)[:, None]
    to_left = mine_step == devices - 1
    rightward_send = mine_step == 1
    pick_left = (ranked(to_left)[None, :] == capacity_ids) & to_left[None, :]
    pick_right = (ranked(rightward_send)[None, :] == capacity_ids) & rightward_send[None, :]
    selector_mask = jnp.concatenate([pick_left, pick_right], axis=0).astype(jnp.bfloat16)
    outgoing = jnp.einsum(
        "sa,ayk->syk", selector_mask, local_tiles, preferred_element_type=jnp.float32
    ).astype(jnp.bfloat16)
    outgoing = outgoing.reshape(2 * CAP * TILE, features)
    extended = extended_2(outgoing, (("dp", 0),), CAP * TILE)
    from_left = extended[: CAP * TILE].reshape(CAP, TILE, features)
    from_right = extended[extended.shape[0] - CAP * TILE :].reshape(CAP, TILE, features)
    candidates = jnp.concatenate([from_left, local_tiles, from_right], axis=0)
    left_marked = left_step == 1
    left_hit = (ranked(left_marked)[None, :] == capacity_ids) & left_marked[None, :]
    left_target = jnp.sum(jnp.where(left_hit, left_slot[None, :], 0), axis=1)
    right_marked = right_step == devices - 1
    right_hit = (ranked(right_marked)[None, :] == capacity_ids) & right_marked[None, :]
    right_target = jnp.sum(jnp.where(right_hit, right_slot[None, :], 0), axis=1)
    target = jnp.concatenate([left_target, mine_slot, right_target])
    usable = jnp.concatenate(
        [jnp.any(left_hit, axis=1), mine_step == 0, jnp.any(right_hit, axis=1)]
    )
    placer = (
        (jnp.arange(tiles_dev, dtype=jnp.int32)[:, None] == target[None, :]) & usable[None, :]
    ).astype(jnp.bfloat16)
    owned_rows = jnp.einsum(
        "sc,crf->srf", placer, candidates, preferred_element_type=jnp.float32
    ).astype(jnp.bfloat16)
    return (sections[None], owned_rows.reshape(tiles_dev * TILE, features))


def solution(mesh):
    in_specs = (
        P("dp", None),
        P("segment", "dp", "mp"),
        P("segment", "dp", "mp"),
        P("segment", "dp", "mp"),
        P("segment", "mp", "dp"),
        P("segment", "mp", "dp"),
        P("segment", "mp", "dp"),
        P("segment", "mp", "dp"),
        P("dp", None),
        P("dp", None),
        P("dp", None),
        P(),
    )
    out_specs = (P("segment", "dp", "mp"), P("dp", ("segment", "mp")))
    return jax.shard_map(
        on_device, mesh=mesh, in_specs=in_specs, out_specs=out_specs, check_vma=False
    )
```

profile of v0, /device:TPU:0, one launch (start us, length us, event | category | flops | bytes accessed | tf_op | source)
XLA Modules:
  0.0 555.2 jit_solution(12145603044757109902)
XLA Ops:
  8.8 2.4 dynamic-slice_select_fusion.2
  11.2 76.6 %all-gather.15.cloned.1.call-done = bf16[1,1024,2048]{2,1,0:T(8,128)(2,1)} async-done(((bf16[1,1024,256]{2,1,0:T(8,128)(2,1)}), bf16[1,1024,2048]{2,1,0:T(8,128)(2,1)}) %all-gather.15.cloned.1.call-update) | async-done | bytes 4194320 | tf_op jit(solution)/shard_map/all_gather | solution.py:122
  87.8 75.3 %all-gather.17.cloned.1.call-done = bf16[1,1024,2048]{2,1,0:T(8,128)(2,1)} async-done(((bf16[1,1024,256]{2,1,0:T(8,128)(2,1)}), bf16[1,1024,2048]{2,1,0:T(8,128)(2,1)}) %all-gather.17.cloned.1.call-update) | async-done | bytes 4194320 | tf_op jit(solution)/shard_map/all_gather | solution.py:123
  163.1 3.0 conditional.3
  166.3 46.4 %reduce-scatter.5.cloned.1.call-done = bf16[256,1024]{1,0:T(8,128)(2,1)} async-done(((bf16[256,2048]{1,0:T(8,128)(2,1)}), bf16[256,1024]{1,0:T(8,128)(2,1)}) %reduce-scatter.5.cloned.1.call-update) | async-done | bytes 524304 | tf_op jit(solution)/shard_map/reduce_scatter | solution.py:160
  213.8 2.4 select_dynamic-update-slice_fusion.7
  216.3 21.4 %all-gather.11.cloned.1.call-done = bf16[256,2048]{1,0:T(8,128)(2,1)} async-done(((bf16[256,1024]{1,0:T(8,128)(2,1)}), bf16[256,2048]{1,0:T(8,128)(2,1)}) %all-gather.11.cloned.1.call-update) | async-done | bytes 1048592 | tf_op jit(solution)/shard_map/all_gather | solution.py:168
  239.4 3.1 collective-permute-done
  242.6 2.9 dynamic-slice_select_fusion.1
  245.5 31.3 %conditional.4 = (bf16[256,2048]{1,0:T(8,128)(2,1)}, bf16[384,1024]{0,1:T(8,128)(2,1)}, bf16[384,1024]{0,1:T(8,128)(2,1)}) conditional(s32[]{:T(128)} %convert_element_type.206, () %tuple.46, (s32[2,2]{1,0:T(2,128)S(1)}, s32[]{:T(128)}, s32[2,2]{1,0:T(2,128)S(1)}, s32[2,2]{1,0:T(2,128)S(1)}, bf16[1,512,1024]{2,1,0:T(8,128)(2,1)}, ...), branch_computations={%region_7.8_spmd, %region_8.13_spmd} | conditional | flops 3363606528 | bytes 75467568 | solution.py:154
  249.1 3.5 constant_dynamic-slice_fusion.6
  252.5 2.3 copy.91
  257.0 3.4 fusion.94
  260.4 4.6 convolution_convert_fusion.3
  267.1 2.5 fusion.21
  273.1 2.3 fusion.98
  276.9 20.4 %reduce-scatter.7.cloned.1.call-done = bf16[256,1024]{1,0:T(8,128)(2,1)} async-done(((bf16[256,2048]{1,0:T(8,128)(2,1)}), bf16[256,1024]{1,0:T(8,128)(2,1)}) %reduce-scatter.7.cloned.1.call-update) | async-done | bytes 524304 | tf_op jit(solution)/shard_map/reduce_scatter | solution.py:160
  297.3 2.7 select_dynamic-update-slice_fusion.6
  301.5 19.9 %all-gather.13.cloned.1.call-done = bf16[256,2048]{1,0:T(8,128)(2,1)} async-done(((bf16[256,1024]{1,0:T(8,128)(2,1)}), bf16[256,2048]{1,0:T(8,128)(2,1)}) %all-gather.13.cloned.1.call-update) | async-done | bytes 1048592 | tf_op jit(solution)/shard_map/all_gather | solution.py:168
  327.3 2.5 select_dynamic-update-slice_fusion.1
  329.8 2.7 select_dynamic-update-slice_fusion.4
  333.9 25.2 %conditional.5 = (bf16[256,2048]{1,0:T(8,128)(2,1)S(1)}, bf16[384,1024]{0,1:T(8,128)(2,1)S(1)}, bf16[384,1024]{0,1:T(8,128)(2,1)S(1)}) conditional(s32[]{:T(128)} %convert_element_type.211, () %tuple.48, (s32[2,2]{1,0:T(2,128)S(1)}, s32[]{:T(128)}, s32[2,2]{1,0:T(2,128)S(1)}, s32[2,2]{1,0:T(2,128)S(1)}, bf16[1,512,1024]{2,1,0:T(8,128)(2,1)}, ...), branch_computations={%region_14.15_spmd, %region_15.20_spmd} | conditional | flops 3363606528 | bytes 90147712 | solution.py:154
  337.6 3.1 constant_dynamic-slice_fusion.12
  345.4 4.4 convolution_convert_fusion.5
  359.1 3.4 select_dynamic-update-slice_fusion
  362.5 36.0 %all-gather.21.cloned.1.call-done = bf16[1,1024,2048]{2,1,0:T(8,128)(2,1)} async-done(((bf16[1,1024,256]{2,1,0:T(8,128)(2,1)}), bf16[1,1024,2048]{2,1,0:T(8,128)(2,1)}) %all-gather.21.cloned.1.call-update) | async-done | bytes 4194320 | tf_op jit(solution)/shard_map/all_gather | solution.py:125
  398.5 8.8 %fusion.51 = f32[768,2048]{1,0:T(8,128)} fusion(bf16[768,1024]{0,1:T(8,128)(2,1)} %get-tuple-element.471, bf16[1,1024,2048]{2,1,0:T(8,128)(2,1)} %all-gather.21.cloned.1.call-done), kind=kOutput, calls=%fused_computation.106 | convolution fusion | flops 3221225472 | bytes 12058624 | tf_op jit(solution)/shard_map/dot_general | solution.py:186
  407.3 66.5 %all-gather.19.cloned.1.call-done = bf16[1,1024,2048]{2,1,0:T(8,128)(2,1)} async-done(((bf16[1,1024,256]{2,1,0:T(8,128)(2,1)}), bf16[1,1024,2048]{2,1,0:T(8,128)(2,1)}) %all-gather.19.cloned.1.call-update) | async-done | bytes 4194320 | tf_op jit(solution)/shard_map/all_gather | solution.py:124
  473.8 9.6 %add_convert_fusion = bf16[768,2048]{1,0:T(8,128)(2,1)} fusion(f32[768,2048]{1,0:T(8,128)} %fusion.51, bf16[768,1024]{0,1:T(8,128)(2,1)} %get-tuple-element.472, bf16[1,1024,2048]{2,1,0:T(8,128)(2,1)} %all-gather.19.cloned.1.call-done), kind=kOutput, calls=%fused_computation.105 | convolution fusion | flops 3224371200 | bytes 15204352 | tf_op jit(solution)/shard_map/dot_general | solution.py:186
  485.4 34.4 %reduce-scatter.11.cloned.1.call-done = bf16[768,512]{1,0:T(8,128)(2,1)} async-done(((bf16[768,2048]{1,0:T(8,128)(2,1)}), bf16[768,512]{1,0:T(8,128)(2,1)}) %reduce-scatter.11.cloned.1.call-update) | async-done | bytes 786448 | tf_op jit(solution)/shard_map/reduce_scatter | solution.py:189
  524.2 3.3 collective-permute-start.3
  528.8 13.4 %reduce-scatter.9.cloned.1.call-done = bf16[256,1024]{1,0:T(8,128)(2,1)} async-done(((bf16[256,2048]{1,0:T(8,128)(2,1)}), bf16[256,1024]{1,0:T(8,128)(2,1)}) %reduce-scatter.9.cloned.1.call-update) | async-done | bytes 524304 | tf_op jit(solution)/shard_map/reduce_scatter | solution.py:160
  (153 shorter events, 59.6 us)
Async XLA Ops:
  7.2 156.0 %copy-start = (bf16[1,768,1024]{2,1,0:T(8,128)(2,1)S(1)}, bf16[1,768,1024]{2,1,0:T(8,128)(2,1)}, u32[]{:S(2)}) copy-start(bf16[1,768,1024]{2,1,0:T(8,128)(2,1)} %param.20) | copy-start | bytes 4718596
  7.2 156.0 %copy-start.1 = (bf16[1,768,1024]{2,1,0:T(8,128)(2,1)S(1)}, bf16[1,768,1024]{2,1,0:T(8,128)(2,1)}, u32[]{:S(2)}) copy-start(bf16[1,768,1024]{2,1,0:T(8,128)(2,1)} %param.21) | copy-start | bytes 4718596
  7.2 155.9 %copy-start.22 = (s32[2,2]{1,0:T(2,128)S(1)}, s32[2,2]{1,0:T(2,128)}, u32[]{:S(2)}) copy-start(s32[2,2]{1,0:T(2,128)} %param.26) | copy-start | bytes 52
  7.2 155.9 %copy-start.23 = (s32[2,2]{1,0:T(2,128)S(1)}, s32[2,2]{1,0:T(2,128)}, u32[]{:S(2)}) copy-start(s32[2,2]{1,0:T(2,128)} %param.27) | copy-start | bytes 52
  7.2 155.9 %copy-start.24 = (s32[2,2]{1,0:T(2,128)S(1)}, s32[2,2]{1,0:T(2,128)}, u32[]{:S(2)}) copy-start(s32[2,2]{1,0:T(2,128)} %param.28) | copy-start | bytes 52
  7.2 80.6 %all-gather.15.cloned.1.call-start = ((), (), s32[]{:S(2)}) async-start(), calls=%async_computation.10 | async-start | bytes 4718592 | tf_op jit(solution)/shard_map/all_gather | solution.py:122
  7.9 155.2 %all-gather.17.cloned.1.call-start = ((), (), s32[]{:S(2)}) async-start(), calls=%async_computation.11 | async-start | bytes 4718592 | tf_op jit(solution)/shard_map/all_gather | solution.py:123
  8.7 204.0 %reduce-scatter.5.cloned.1.call-start = ((), (), s32[]{:S(2)}) async-start(), calls=%async_computation.4 | async-start | bytes 1572864 | tf_op jit(solution)/shard_map/reduce_scatter | solution.py:160
  166.2 71.5 %all-gather.11.cloned.1.call-start = ((), (), s32[]{:S(2)}) async-start(), calls=%async_computation.5 | async-start | bytes 1572864 | tf_op jit(solution)/shard_map/all_gather | solution.py:168
  216.2 81.1 %reduce-scatter.7.cloned.1.call-start = ((), (), s32[]{:S(2)}) async-start(), calls=%async_computation.6 | async-start | bytes 1572864 | tf_op jit(solution)/shard_map/reduce_scatter | solution.py:160
  237.7 4.9 collective-permute-start
  267.1 2.5 copy-start.16
  267.1 2.5 copy-start.19
  267.1 2.7 copy-start.30
  269.7 3.3 copy-start.27
  276.8 44.6 %all-gather.13.cloned.1.call-start = ((), (), s32[]{:S(2)}) async-start(), calls=%async_computation.7 | async-start | bytes 1572864 | tf_op jit(solution)/shard_map/all_gather | solution.py:168
  300.0 98.6 %all-gather.21.cloned.1.call-start = ((), (), s32[]{:S(2)}) async-start(), calls=%async_computation.13 | async-start | bytes 4718592 | tf_op jit(solution)/shard_map/all_gather | solution.py:125
  300.7 173.1 %all-gather.19.cloned.1.call-start = ((), (), s32[]{:S(2)}) async-start(), calls=%async_computation.12 | async-start | bytes 4718592 | tf_op jit(solution)/shard_map/all_gather | solution.py:124
  301.5 218.3 %reduce-scatter.11.cloned.1.call-start = ((), (), s32[]{:S(2)}) async-start(), calls=%async_computation.9 | async-start | bytes 3932160 | tf_op jit(solution)/shard_map/reduce_scatter | solution.py:189
  321.4 11.1 %collective-permute-start.1 = (bf16[256,2048]{1,0:T(8,128)(2,1)}, bf16[256,2048]{1,0:T(8,128)(2,1)S(1)}, u32[]{:S(2)}, u32[]{:S(2)}) collective-permute-start(bf16[256,2048]{1,0:T(8,128)(2,1)} %all-gather.13.cloned.1.call-done), channel_id=1, source_target_pairs={{16,0},{17,1},{18,2},{19,3},{20,4},{21,5},{22,6},{23,7},{24,8},{25... | collective-permute-start | bytes 3145736 | tf_op jit(solution)/shard_map/ppermute | solution.py:15
  329.8 2.7 copy-start.3
  337.6 3.1 copy-start.2
  340.8 2.6 copy-start.9
  345.4 5.6 %copy-start.17 = (bf16[1,384,1024]{1,2,0:T(8,128)(2,1)S(1)}, bf16[1,384,1024]{1,2,0:T(8,128)(2,1)}, u32[]{:S(2)}) copy-start(bf16[1,384,1024]{1,2,0:T(8,128)(2,1)} %get-tuple-element.457) | copy-start | bytes 2359300 | tf_op jit(solution)/shard_map/cond
  351.1 2.2 copy-start.20
  351.1 2.2 copy-start.31
  359.1 3.4 copy-start.5
  483.5 58.8 %reduce-scatter.9.cloned.1.call-start = ((), (), s32[]{:S(2)}) async-start(), calls=%async_computation.8 | async-start | bytes 1572864 | tf_op jit(solution)/shard_map/reduce_scatter | solution.py:160
  521.9 20.4 %copy-start.10 = (bf16[256,2048]{1,0:T(8,128)(2,1)S(1)}, bf16[256,2048]{1,0:T(8,128)(2,1)}, u32[]{:S(2)}) copy-start(bf16[256,2048]{1,0:T(8,128)(2,1)} %dynamic-slice_select_fusion) | copy-start | bytes 3145732
  521.9 22.3 %collective-permute-start.2 = (bf16[256,512]{1,0:T(8,128)(2,1)S(1)}, bf16[256,512]{1,0:T(8,128)(2,1)S(1)}, u32[]{:S(2)}, u32[]{:S(2)}) collective-permute-start(bf16[256,512]{1,0:T(8,128)(2,1)S(1)} %bitcast.229), channel_id=1, source_target_pairs={{0,2},{2,4},{4,6},{6,8},{8,10},{10,12},{12,14},{14,0},{1,3},{3,5},... | collective-permute-start | bytes 786440 | tf_op jit(solution)/shard_map/ppermute | solution.py:24
  524.2 20.4 %collective-permute-start.3 = (bf16[256,512]{1,0:T(8,128)(2,1)}, bf16[256,512]{1,0:T(8,128)(2,1)}, u32[]{:S(2)}, u32[]{:S(2)}) collective-permute-start(bf16[256,512]{1,0:T(8,128)(2,1)} %bitcast.62), channel_id=1, source_target_pairs={{2,0},{4,2},{6,4},{8,6},{10,8},{12,10},{14,12},{0,14},{3,1},{5,3},... | collective-permute-start | bytes 786440 | tf_op jit(solution)/shard_map/ppermute | solution.py:27
  528.8 14.9 %copy-start.4 = (bf16[768,512]{1,0:T(8,128)(2,1)S(1)}, bf16[768,512]{1,0:T(8,128)(2,1)}, u32[]{:S(2)}) copy-start(bf16[768,512]{1,0:T(8,128)(2,1)} %reduce-scatter.11.cloned.1.call-done) | copy-start | bytes 2359300
  (8 other events, 11.6 us)
Sparse Core Ops, SparseCore 0:
  10.1 77.7 all-gather.14
  89.9 73.1 all-gather.16
  166.3 46.3 reduce-scatter.4
  216.3 21.3 all-gather.10
  276.9 20.3 reduce-scatter.6
  300.1 21.2 all-gather.12
  323.5 75.0 all-gather.20
  400.6 73.1 all-gather.18
  483.6 36.0 reduce-scatter.10
  521.9 20.3 reduce-scatter.8
where the time goes:
time: 563 us; the launch traced here: 555 us
  waiting for transfers between devices  416 us (74%)
  matrix products  50.6 us (9%)
  local copies, waits for them, and re-layouts  39 us (7%)
  other arithmetic  25.7 us (5%)
  between operations  14.7 us (3%)
  starting transfers between devices  8.2 us (1%)
    reduce_scatter x3, waiting for transfers between devices, on_device(): lax.psum_scatter(mixed_grad.astype(jnp.bfloat16), 'mp', scatter_dimension...  80.3 us
    all_gather x1, waiting for transfers between devices, on_device(): lax.all_gather(w_out[0], 'dp', axis=1, tiled=True)  76.6 us
    all_gather x1, waiting for transfers between devices, on_device(): lax.all_gather(w_query[0], 'dp', axis=1, tiled=True)  75.3 us
    all_gather x1, waiting for transfers between devices, on_device(): lax.all_gather(w_key[0], 'dp', axis=1, tiled=True)  66.5 us
    all_gather x2, waiting for transfers between devices, on_device(): full_section = lax.all_gather(own_section, 'mp', axis=1, tiled=True)  41.3 us
    all_gather x1, waiting for transfers between devices, on_device(): lax.all_gather(w_value[0], 'dp', axis=1, tiled=True)  36 us
    reduce_scatter x1, waiting for transfers between devices, on_device(): lax.psum_scatter(encoder_partial.astype(jnp.bfloat16), ('segment', 'mp'),...  34.4 us
    another operation x11, local copies, waits for them, and re-layouts  15.5 us
  transfers between devices with their start and end apart: 14, of which 11 were waited for; matrix products, arithmetic and copies ran while one was open for 10% of the time, Pallas kernels for 0%

commit v1 on v0

--- a/solution.py
+++ b/solution.py
@@ -2,11 +2,30 @@
 import jax.numpy as jnp
 from jax import lax
 from jax.sharding import PartitionSpec as P
+from jax.lax import axis_index, axis_size, ppermute
 
 DH = 256
 TILE = 128
 CAP = 2
 masked_floor = -1e30
+
+
+def watch_records(s0):
+    a_name = "dp"
+    cores_n = axis_size(a_name)
+    crops = tuple(((dev_i, (dev_i + 1) % cores_n) for dev_i in range(cores_n)))
+    history = tuple(((dev_i, (dev_i - 1) % cores_n) for dev_i in range(cores_n)))
+    left_arr, out_arr = ([s0], [s0])
+    for _ in range(cores_n // 2):
+        left_arr.append(ppermute(left_arr[-1], a_name, perm=crops))
+    for _ in range((cores_n - 1) // 2):
+        out_arr.append(ppermute(out_arr[-1], a_name, history))
+    big = jnp.roll(
+        jnp.concatenate([*left_arr[::-1], *out_arr[1:]], 1),
+        (axis_index(a_name) - cores_n // 2) * s0.shape[1],
+        1,
+    )
+    return big
 
 
 def shifted(block, axis, distance):
@@ -119,7 +138,7 @@
     local_width = saved_query.shape[2]
     half_width = width // lax.axis_size("mp")
     out_full, query_full, key_full, complete_value = (
-        lax.all_gather(w_out[0], "dp", axis=1, tiled=True),
+        watch_records(w_out[0]),
         lax.all_gather(w_query[0], "dp", axis=1, tiled=True),
         lax.all_gather(w_key[0], "dp", axis=1, tiled=True),
         lax.all_gather(w_value[0], "dp", axis=1, tiled=True),

time: 563 us -> 537 us (0.954)
  waiting for transfers between devices: 416 us -> 370 us
  starting transfers between devices: 8.2 us -> 25.7 us
    ppermute x0 -> x7, waiting for transfers between devices: none -> 91.1 us  [the longest x4 88 us: watch_records(): left_arr.append(ppermute(left_arr[-1], a_name, perm=crops))]
    all_gather x1 -> x0, waiting for transfers between devices: 76.6 us -> none  [on_device(): lax.all_gather(w_out[0], 'dp', axis=1, tiled=True)]
    all_gather x1, waiting for transfers between devices: 75.3 us -> 13.4 us  [on_device(): lax.all_gather(w_query[0], 'dp', axis=1, tiled=True)]
    ppermute x0 -> x7, starting transfers between devices: none -> 17.6 us  [the longest x3 9.33 us: watch_records(): out_arr.append(ppermute(out_arr[-1], a_name, history))]
  transfers between devices with their start and end apart: 14 -> 20, of which waited for: 11 -> 16; matrix products, arithmetic and copies ran while one was open for 10% -> 11% of each run, Pallas kernels for 0% -> 0%
where the time goes in v1:
time: 537 us; the launch traced here: 528 us
  waiting for transfers between devices  370 us (69%)
  matrix products  51.5 us (10%)
  local copies, waits for them, and re-layouts  40.1 us (7%)
  other arithmetic  26 us (5%)
  starting transfers between devices  25.7 us (5%)
  between operations  14.5 us (3%)
    ppermute x4, waiting for transfers between devices, watch_records(): left_arr.append(ppermute(left_arr[-1], a_name, perm=crops))  88 us
    reduce_scatter x3, waiting for transfers between devices, on_device(): lax.psum_scatter(mixed_grad.astype(jnp.bfloat16), 'mp', scatter_dimension...  80.1 us
    all_gather x1, waiting for transfers between devices, on_device(): lax.all_gather(w_key[0], 'dp', axis=1, tiled=True)  66.5 us
    all_gather x2, waiting for transfers between devices, on_device(): full_section = lax.all_gather(own_section, 'mp', axis=1, tiled=True)  41.5 us
    all_gather x1, waiting for transfers between devices, on_device(): lax.all_gather(w_value[0], 'dp', axis=1, tiled=True)  37.7 us
    reduce_scatter x1, waiting for transfers between devices, on_device(): lax.psum_scatter(encoder_partial.astype(jnp.bfloat16), ('segment', 'mp'),...  34.4 us
    another operation x11, local copies, waits for them, and re-layouts  14.8 us
    all_gather x1, waiting for transfers between devices, on_device(): lax.all_gather(w_query[0], 'dp', axis=1, tiled=True)  13.4 us
  transfers between devices with their start and end apart: 20, of which 16 were waited for; matrix products, arithmetic and copies ran while one was open for 11% of the time, Pallas kernels for 0%

profile of v1, /device:TPU:0, one launch (start us, length us, event | category | flops | bytes accessed | tf_op | source)
XLA Modules:
  0.0 528.2 jit_solution(4060708506837453270)
XLA Ops:
  7.9 3.0 collective-permute-start
  10.9 15.4 %collective-permute-done = bf16[1024,256]{1,0:T(8,128)(2,1)S(1)} collective-permute-done((bf16[1024,256]{1,0:T(8,128)(2,1)}, bf16[1024,256]{1,0:T(8,128)(2,1)S(1)}, u32[]{:S(2)}, u32[]{:S(2)}) %collective-permute-start) | collective-permute-done | bytes 524320 | tf_op jit(solution)/shard_map/ppermute | solution.py:20
  26.6 4.4 collective-permute-start.4
  31.0 19.4 %collective-permute-done.1 = bf16[1024,256]{1,0:T(8,128)(2,1)S(1)} collective-permute-done((bf16[1024,256]{1,0:T(8,128)(2,1)S(1)}, bf16[1024,256]{1,0:T(8,128)(2,1)S(1)}, u32[]{:S(2)}, u32[]{:S(2)}) %collective-permute-start.1) | collective-permute-done | bytes 524320 | tf_op jit(solution)/shard_map/ppermute | solution.py:20
  55.9 25.9 %collective-permute-done.2 = bf16[1024,256]{1,0:T(8,128)(2,1)S(1)} collective-permute-done((bf16[1024,256]{1,0:T(8,128)(2,1)S(1)}, bf16[1024,256]{1,0:T(8,128)(2,1)S(1)}, u32[]{:S(2)}, u32[]{:S(2)}) %collective-permute-start.2) | collective-permute-done | bytes 524320 | tf_op jit(solution)/shard_map/ppermute | solution.py:20
  86.8 3.1 collective-permute-start.6
  90.0 27.3 %collective-permute-done.3 = bf16[1024,256]{1,0:T(8,128)(2,1)S(1)} collective-permute-done((bf16[1024,256]{1,0:T(8,128)(2,1)S(1)}, bf16[1024,256]{1,0:T(8,128)(2,1)S(1)}, u32[]{:S(2)}, u32[]{:S(2)}) %collective-permute-start.3) | collective-permute-done | bytes 524320 | tf_op jit(solution)/shard_map/ppermute | solution.py:20
  123.5 13.4 %all-gather.13.cloned.1.call-done = bf16[1,1024,2048]{2,1,0:T(8,128)(2,1)} async-done(((bf16[1,1024,256]{2,1,0:T(8,128)(2,1)}), bf16[1,1024,2048]{2,1,0:T(8,128)(2,1)}) %all-gather.13.cloned.1.call-update) | async-done | bytes 4194320 | tf_op jit(solution)/shard_map/all_gather | solution.py:142
  137.0 3.0 conditional.3
  140.1 46.1 %reduce-scatter.5.cloned.1.call-done = bf16[256,1024]{1,0:T(8,128)(2,1)} async-done(((bf16[256,2048]{1,0:T(8,128)(2,1)}), bf16[256,1024]{1,0:T(8,128)(2,1)}) %reduce-scatter.5.cloned.1.call-update) | async-done | bytes 524304 | tf_op jit(solution)/shard_map/reduce_scatter | solution.py:179
  189.8 21.4 %all-gather.9.cloned.1.call-done = bf16[256,2048]{1,0:T(8,128)(2,1)} async-done(((bf16[256,1024]{1,0:T(8,128)(2,1)}), bf16[256,2048]{1,0:T(8,128)(2,1)}) %all-gather.9.cloned.1.call-update) | async-done | bytes 1048592 | tf_op jit(solution)/shard_map/all_gather | solution.py:187
  212.9 3.1 collective-permute-done.7
  216.1 3.0 dynamic-slice_select_fusion.1
  219.0 31.3 %conditional.4 = (bf16[256,2048]{1,0:T(8,128)(2,1)}, bf16[384,1024]{0,1:T(8,128)(2,1)}, bf16[384,1024]{0,1:T(8,128)(2,1)}) conditional(s32[]{:T(128)} %convert_element_type.206, () %tuple.46, (s32[2,2]{1,0:T(2,128)S(1)}, s32[]{:T(128)}, s32[2,2]{1,0:T(2,128)S(1)}, s32[2,2]{1,0:T(2,128)S(1)}, bf16[1,512,1024]{2,1,0:T(8,128)(2,1)}, ...), branch_computations={%region_7.8_spmd, %region_8.13_spmd} | conditional | flops 3363606528 | bytes 75467568 | solution.py:173
  222.5 3.5 constant_dynamic-slice_fusion.6
  230.5 3.4 fusion.94
  233.9 4.6 convolution_convert_fusion.3
  250.4 20.4 %reduce-scatter.7.cloned.1.call-done = bf16[256,1024]{1,0:T(8,128)(2,1)} async-done(((bf16[256,2048]{1,0:T(8,128)(2,1)}), bf16[256,1024]{1,0:T(8,128)(2,1)}) %reduce-scatter.7.cloned.1.call-update) | async-done | bytes 524304 | tf_op jit(solution)/shard_map/reduce_scatter | solution.py:179
  270.8 2.7 select_dynamic-update-slice_fusion.6
  274.9 20.1 %all-gather.11.cloned.1.call-done = bf16[256,2048]{1,0:T(8,128)(2,1)} async-done(((bf16[256,1024]{1,0:T(8,128)(2,1)}), bf16[256,2048]{1,0:T(8,128)(2,1)}) %all-gather.11.cloned.1.call-update) | async-done | bytes 1048592 | tf_op jit(solution)/shard_map/all_gather | solution.py:187
  303.5 2.8 select_dynamic-update-slice_fusion.1
  307.7 22.9 %conditional.5 = (bf16[256,2048]{1,0:T(8,128)(2,1)}, bf16[384,1024]{0,1:T(8,128)(2,1)}, bf16[384,1024]{0,1:T(8,128)(2,1)}) conditional(s32[]{:T(128)} %convert_element_type.211, () %tuple.48, (s32[2,2]{1,0:T(2,128)S(1)}, s32[]{:T(128)}, s32[2,2]{1,0:T(2,128)S(1)}, s32[2,2]{1,0:T(2,128)S(1)}, bf16[1,512,1024]{2,1,0:T(8,128)(2,1)}, ...), branch_computations={%region_14.15_spmd, %region_15.20_spmd} | conditional | flops 3363606528 | bytes 85953360 | solution.py:173
  311.4 3.1 constant_dynamic-slice_fusion.12
  317.7 3.5 convolution_convert_fusion.5
  330.6 3.5 select_dynamic-update-slice_fusion
  334.1 37.7 %all-gather.17.cloned.1.call-done = bf16[1,1024,2048]{2,1,0:T(8,128)(2,1)} async-done(((bf16[1,1024,256]{2,1,0:T(8,128)(2,1)}), bf16[1,1024,2048]{2,1,0:T(8,128)(2,1)}) %all-gather.17.cloned.1.call-update) | async-done | bytes 4194320 | tf_op jit(solution)/shard_map/all_gather | solution.py:144
  371.9 8.8 %fusion.51 = f32[768,2048]{1,0:T(8,128)} fusion(bf16[768,1024]{0,1:T(8,128)(2,1)} %get-tuple-element.471, bf16[1,1024,2048]{2,1,0:T(8,128)(2,1)} %all-gather.17.cloned.1.call-done), kind=kOutput, calls=%fused_computation.106 | convolution fusion | flops 3221225472 | bytes 12058624 | tf_op jit(solution)/shard_map/dot_general | solution.py:205
  380.7 66.5 %all-gather.15.cloned.1.call-done = bf16[1,1024,2048]{2,1,0:T(8,128)(2,1)} async-done(((bf16[1,1024,256]{2,1,0:T(8,128)(2,1)}), bf16[1,1024,2048]{2,1,0:T(8,128)(2,1)}) %all-gather.15.cloned.1.call-update) | async-done | bytes 4194320 | tf_op jit(solution)/shard_map/all_gather | solution.py:143
  447.1 9.6 %add_convert_fusion = bf16[768,2048]{1,0:T(8,128)(2,1)} fusion(f32[768,2048]{1,0:T(8,128)} %fusion.51, bf16[768,1024]{0,1:T(8,128)(2,1)} %get-tuple-element.472, bf16[1,1024,2048]{2,1,0:T(8,128)(2,1)} %all-gather.15.cloned.1.call-done), kind=kOutput, calls=%fused_computation.105 | convolution fusion | flops 3224371200 | bytes 15204352 | tf_op jit(solution)/shard_map/dot_general | solution.py:205
  458.7 34.4 %reduce-scatter.11.cloned.1.call-done = bf16[768,512]{1,0:T(8,128)(2,1)} async-done(((bf16[768,2048]{1,0:T(8,128)(2,1)}), bf16[768,512]{1,0:T(8,128)(2,1)}) %reduce-scatter.11.cloned.1.call-update) | async-done | bytes 786448 | tf_op jit(solution)/shard_map/reduce_scatter | solution.py:208
  497.6 3.2 collective-permute-start.10
  502.3 13.5 %reduce-scatter.9.cloned.1.call-done = bf16[256,1024]{1,0:T(8,128)(2,1)} async-done(((bf16[256,2048]{1,0:T(8,128)(2,1)}), bf16[256,1024]{1,0:T(8,128)(2,1)}) %reduce-scatter.9.cloned.1.call-update) | async-done | bytes 524304 | tf_op jit(solution)/shard_map/reduce_scatter | solution.py:179
  (177 shorter events, 86.2 us)
Async XLA Ops:
  7.2 129.8 %all-gather.13.cloned.1.call-start = ((), (), s32[]{:S(2)}) async-start(), calls=%async_computation.10 | async-start | bytes 4718592 | tf_op jit(solution)/shard_map/all_gather | solution.py:142
  7.9 178.3 %reduce-scatter.5.cloned.1.call-start = ((), (), s32[]{:S(2)}) async-start(), calls=%async_computation.4 | async-start | bytes 1572864 | tf_op jit(solution)/shard_map/reduce_scatter | solution.py:179
  7.9 18.4 %collective-permute-start = (bf16[1024,256]{1,0:T(8,128)(2,1)}, bf16[1024,256]{1,0:T(8,128)(2,1)S(1)}, u32[]{:S(2)}, u32[]{:S(2)}) collective-permute-start(bf16[1024,256]{1,0:T(8,128)(2,1)} %bitcast.204), channel_id=1, source_target_pairs={{0,2},{2,4},{4,6},{6,8},{8,10},{10,12},{12,14},{14,0},{1,3},{3,5},... | collective-permute-start | bytes 1572872 | tf_op jit(solution)/shard_map/ppermute | solution.py:20
  26.3 24.1 %collective-permute-start.1 = (bf16[1024,256]{1,0:T(8,128)(2,1)S(1)}, bf16[1024,256]{1,0:T(8,128)(2,1)S(1)}, u32[]{:S(2)}, u32[]{:S(2)}) collective-permute-start(bf16[1024,256]{1,0:T(8,128)(2,1)S(1)} %collective-permute-done), channel_id=1, source_target_pairs={{0,2},{2,4},{4,6},{6,8},{8,10},{10,12},{12,14},{14,0},{1,3},{3,5},... | collective-permute-start | bytes 1572872 | tf_op jit(solution)/shard_map/ppermute | solution.py:20
  26.6 27.6 %collective-permute-start.4 = (bf16[1024,256]{1,0:T(8,128)(2,1)}, bf16[1024,256]{1,0:T(8,128)(2,1)S(1)}, u32[]{:S(2)}, u32[]{:S(2)}) collective-permute-start(bf16[1024,256]{1,0:T(8,128)(2,1)} %bitcast.205), channel_id=1, source_target_pairs={{0,14},{2,0},{4,2},{6,4},{8,6},{10,8},{12,10},{14,12},{1,15},{3,1}... | collective-permute-start | bytes 1572872 | tf_op jit(solution)/shard_map/ppermute | solution.py:22
  50.4 31.5 %collective-permute-start.2 = (bf16[1024,256]{1,0:T(8,128)(2,1)S(1)}, bf16[1024,256]{1,0:T(8,128)(2,1)S(1)}, u32[]{:S(2)}, u32[]{:S(2)}) collective-permute-start(bf16[1024,256]{1,0:T(8,128)(2,1)S(1)} %collective-permute-done.1), channel_id=1, source_target_pairs={{0,2},{2,4},{4,6},{6,8},{8,10},{10,12},{12,14},{14,0},{1,3},{3,5},... | collective-permute-start | bytes 1572872 | tf_op jit(solution)/shard_map/ppermute | solution.py:20
  54.2 32.6 %collective-permute-start.5 = (bf16[1024,256]{1,0:T(8,128)(2,1)S(1)}, bf16[1024,256]{1,0:T(8,128)(2,1)S(1)}, u32[]{:S(2)}, u32[]{:S(2)}) collective-permute-start(bf16[1024,256]{1,0:T(8,128)(2,1)S(1)} %collective-permute-done.4), channel_id=1, source_target_pairs={{0,14},{2,0},{4,2},{6,4},{8,6},{10,8},{12,10},{14,12},{1,15},{3,1}... | collective-permute-start | bytes 1572872 | tf_op jit(solution)/shard_map/ppermute | solution.py:22
  81.9 35.4 %collective-permute-start.3 = (bf16[1024,256]{1,0:T(8,128)(2,1)S(1)}, bf16[1024,256]{1,0:T(8,128)(2,1)S(1)}, u32[]{:S(2)}, u32[]{:S(2)}) collective-permute-start(bf16[1024,256]{1,0:T(8,128)(2,1)S(1)} %collective-permute-done.2), channel_id=1, source_target_pairs={{0,2},{2,4},{4,6},{6,8},{8,10},{10,12},{12,14},{14,0},{1,3},{3,5},... | collective-permute-start | bytes 1572872 | tf_op jit(solution)/shard_map/ppermute | solution.py:20
  86.8 33.6 %collective-permute-start.6 = (bf16[1024,256]{1,0:T(8,128)(2,1)S(1)}, bf16[1024,256]{1,0:T(8,128)(2,1)S(1)}, u32[]{:S(2)}, u32[]{:S(2)}) collective-permute-start(bf16[1024,256]{1,0:T(8,128)(2,1)S(1)} %collective-permute-done.5), channel_id=1, source_target_pairs={{0,14},{2,0},{4,2},{6,4},{8,6},{10,8},{12,10},{14,12},{1,15},{3,1}... | collective-permute-start | bytes 1572872 | tf_op jit(solution)/shard_map/ppermute | solution.py:22
  121.0 15.9 %copy-start = (bf16[1,768,1024]{2,1,0:T(8,128)(2,1)S(1)}, bf16[1,768,1024]{2,1,0:T(8,128)(2,1)}, u32[]{:S(2)}) copy-start(bf16[1,768,1024]{2,1,0:T(8,128)(2,1)} %param.20) | copy-start | bytes 4718596
  121.0 15.9 %copy-start.1 = (bf16[1,768,1024]{2,1,0:T(8,128)(2,1)S(1)}, bf16[1,768,1024]{2,1,0:T(8,128)(2,1)}, u32[]{:S(2)}) copy-start(bf16[1,768,1024]{2,1,0:T(8,128)(2,1)} %param.21) | copy-start | bytes 4718596
  121.0 15.9 %copy-start.20 = (s32[2,2]{1,0:T(2,128)S(1)}, s32[2,2]{1,0:T(2,128)}, u32[]{:S(2)}) copy-start(s32[2,2]{1,0:T(2,128)} %param.26) | copy-start | bytes 52
  121.1 15.9 %copy-start.21 = (s32[2,2]{1,0:T(2,128)S(1)}, s32[2,2]{1,0:T(2,128)}, u32[]{:S(2)}) copy-start(s32[2,2]{1,0:T(2,128)} %param.27) | copy-start | bytes 52
  121.1 15.9 %copy-start.22 = (s32[2,2]{1,0:T(2,128)S(1)}, s32[2,2]{1,0:T(2,128)}, u32[]{:S(2)}) copy-start(s32[2,2]{1,0:T(2,128)} %param.28) | copy-start | bytes 52
  140.0 71.1 %all-gather.9.cloned.1.call-start = ((), (), s32[]{:S(2)}) async-start(), calls=%async_computation.5 | async-start | bytes 1572864 | tf_op jit(solution)/shard_map/all_gather | solution.py:187
  189.7 81.1 %reduce-scatter.7.cloned.1.call-start = ((), (), s32[]{:S(2)}) async-start(), calls=%async_computation.6 | async-start | bytes 1572864 | tf_op jit(solution)/shard_map/reduce_scatter | solution.py:179
  211.2 4.9 collective-permute-start.7
  240.6 2.7 copy-start.28
  243.2 3.3 copy-start.25
  250.3 44.6 %all-gather.11.cloned.1.call-start = ((), (), s32[]{:S(2)}) async-start(), calls=%async_computation.7 | async-start | bytes 1572864 | tf_op jit(solution)/shard_map/all_gather | solution.py:187
  273.5 98.4 %all-gather.17.cloned.1.call-start = ((), (), s32[]{:S(2)}) async-start(), calls=%async_computation.12 | async-start | bytes 4718592 | tf_op jit(solution)/shard_map/all_gather | solution.py:144
  274.0 173.1 %all-gather.15.cloned.1.call-start = ((), (), s32[]{:S(2)}) async-start(), calls=%async_computation.11 | async-start | bytes 4718592 | tf_op jit(solution)/shard_map/all_gather | solution.py:143
  274.8 218.3 %reduce-scatter.11.cloned.1.call-start = ((), (), s32[]{:S(2)}) async-start(), calls=%async_computation.9 | async-start | bytes 3932160 | tf_op jit(solution)/shard_map/reduce_scatter | solution.py:208
  294.9 11.4 %collective-permute-start.8 = (bf16[256,2048]{1,0:T(8,128)(2,1)}, bf16[256,2048]{1,0:T(8,128)(2,1)S(1)}, u32[]{:S(2)}, u32[]{:S(2)}) collective-permute-start(bf16[256,2048]{1,0:T(8,128)(2,1)} %all-gather.11.cloned.1.call-done), channel_id=1, source_target_pairs={{16,0},{17,1},{18,2},{19,3},{20,4},{21,5},{22,6},{23,7},{24,8},{25... | collective-permute-start | bytes 3145736 | tf_op jit(solution)/shard_map/ppermute | solution.py:34
  303.5 2.8 copy-start.3
  311.4 3.1 copy-start.2
  456.8 59.0 %reduce-scatter.9.cloned.1.call-start = ((), (), s32[]{:S(2)}) async-start(), calls=%async_computation.8 | async-start | bytes 1572864 | tf_op jit(solution)/shard_map/reduce_scatter | solution.py:179
  495.2 20.6 %copy-start.9 = (bf16[256,2048]{1,0:T(8,128)(2,1)S(1)}, bf16[256,2048]{1,0:T(8,128)(2,1)}, u32[]{:S(2)}) copy-start(bf16[256,2048]{1,0:T(8,128)(2,1)} %dynamic-slice_select_fusion) | copy-start | bytes 3145732
  495.3 22.5 %collective-permute-start.9 = (bf16[256,512]{1,0:T(8,128)(2,1)S(1)}, bf16[256,512]{1,0:T(8,128)(2,1)S(1)}, u32[]{:S(2)}, u32[]{:S(2)}) collective-permute-start(bf16[256,512]{1,0:T(8,128)(2,1)S(1)} %bitcast.231), channel_id=1, source_target_pairs={{0,2},{2,4},{4,6},{6,8},{8,10},{10,12},{12,14},{14,0},{1,3},{3,5},... | collective-permute-start | bytes 786440 | tf_op jit(solution)/shard_map/ppermute | solution.py:43
  497.6 20.5 %collective-permute-start.10 = (bf16[256,512]{1,0:T(8,128)(2,1)}, bf16[256,512]{1,0:T(8,128)(2,1)}, u32[]{:S(2)}, u32[]{:S(2)}) collective-permute-start(bf16[256,512]{1,0:T(8,128)(2,1)} %bitcast.62), channel_id=1, source_target_pairs={{2,0},{4,2},{6,4},{8,6},{10,8},{12,10},{14,12},{0,14},{3,1},{5,3},... | collective-permute-start | bytes 786440 | tf_op jit(solution)/shard_map/ppermute | solution.py:46
  502.3 15.0 %copy-start.4 = (bf16[768,512]{1,0:T(8,128)(2,1)S(1)}, bf16[768,512]{1,0:T(8,128)(2,1)}, u32[]{:S(2)}) copy-start(bf16[768,512]{1,0:T(8,128)(2,1)} %reduce-scatter.11.cloned.1.call-done) | copy-start | bytes 2359300
  517.3 3.0 copy-start.14
  (12 other events, 21.5 us)
Sparse Core Ops, SparseCore 0:
  10.0 126.8 all-gather.12
  140.2 45.9 reduce-scatter.4
  189.8 21.2 all-gather.8
  250.4 20.3 reduce-scatter.6
  273.6 21.2 all-gather.10
  296.8 75.0 all-gather.16
  373.9 73.1 all-gather.14
  456.9 36.1 reduce-scatter.10
  495.4 20.3 reduce-scatter.8
